TPU v7x, 256 devices: a whole 4x4x8 slice. The times are simulated.
256 devices in a mesh: dp: 2 (over z_hi), row: 32 (over y, x, core), col: 4 (over z_lo).
Axes of the slice: x: 4, y: 4, z: 8 (z_hi: 2, z_lo: 4; z = z_hi * 4 + z_lo), core: 2. Of those that a mesh axis runs over, the one named last changes fastest.
Arguments:
- saved_input: bfloat16 [24576, 2048], P(('dp', 'row'), 'col'), may hold values from -16 to 16
- cotangent: bfloat16 [24576, 2048], P(('dp', 'row'), 'col'), may hold values from -16 to 16
- weight_in: bfloat16 [2048, 4096], P('row', 'col'), may hold values from -0.125 to 0.125
- weight_out: bfloat16 [4096, 2048], P('col', 'row'), may hold values from -0.09375 to 0.09375
- in_row_moment: float32 [2048], P('row'), may hold values from 96 to 6144
- in_col_moment: float32 [4096], P('col'), may hold values from 96 to 6144
- out_row_moment: float32 [4096], P('col'), may hold values from 98304 to 1572864
- out_col_moment: float32 [2048], P('row'), may hold values from 98304 to 1572864
Outputs:
- input_grad: bfloat16 [24576, 2048], P(('dp', 'row'), 'col')
- in_update: float32 [2048, 4096], P('row', 'col')
- out_update: float32 [4096, 2048], P('col', 'row')
- in_row_new: float32 [2048], P('row')
- in_col_new: float32 [4096], P('col')
- out_row_new: float32 [4096], P('col')
- out_col_new: float32 [2048], P('row')
All inputs are finite; a program needn't handle non-finite values.
Results may differ from a plain program's by a relative error of at most 0.0049.
Values may be sent and summed in bfloat16 or wider, within the bound.
A program may use at most 128 MiB of HBM per device.

v0:
```python
import jax
import jax.numpy as jnp
from jax import lax
from jax.sharding import PartitionSpec as P

GELU_SCALE = 0.7978845608028654
GELU_CUBIC = 0.044715
MOMENT_DECAY = 0.8
CLIP_LIMIT = 1.0
EPSILON_SQ = 1e-30


def gelu_parts(values):
    inner = GELU_SCALE * (values + GELU_CUBIC * values * values * values)
    tangent = jnp.tanh(inner)
    output = 0.5 * values * (1.0 + tangent)
    slope = 0.5 * (1.0 + tangent) + 0.5 * values * (1.0 - tangent * tangent) * GELU_SCALE * (
        1.0 + 3.0 * GELU_CUBIC * values * values
    )
    return (output, slope)


def moment_mix(old_values, sums, divisor):
    return MOMENT_DECAY * old_values + (1.0 - MOMENT_DECAY) * (sums / divisor + EPSILON_SQ)


def local(
    saved_input,
    cotangent,
    weight_in,
    weight_out,
    in_row_moment,
    in_col_moment,
    out_row_moment,
    out_col_moment,
):
    full_input, full_cotangent = (
        lax.all_gather(saved_input, "col", axis=1, tiled=True),
        lax.all_gather(cotangent, "col", axis=1, tiled=True),
    )
    full_weight_in, full_weight_out = (
        lax.all_gather(weight_in, "row", axis=0, tiled=True),
        lax.all_gather(weight_out, "row", axis=1, tiled=True),
    )
    preact = jnp.dot(full_input, full_weight_in, preferred_element_type=jnp.float32)
    output, slope = gelu_parts(preact)
    hidden = output.astype(jnp.bfloat16)
    hidden_grad = lax.dot_general(
        full_cotangent,
        full_weight_out,
        (((1,), (1,)), ((), ())),
        preferred_element_type=jnp.float32,
    )
    preact_grad = (hidden_grad * slope).astype(jnp.bfloat16)
    input_terms = lax.dot_general(
        preact_grad, full_weight_in, (((1,), (1,)), ((), ())), preferred_element_type=jnp.float32
    )
    input_grad = lax.psum_scatter(input_terms, "col", scatter_dimension=1, tiled=True).astype(
        jnp.bfloat16
    )
    model_width = full_input.shape[1]
    local_units = full_weight_in.shape[1]
    hidden_units = local_units * lax.axis_size("col")
    first_term = lax.dot_general(
        full_input, preact_grad, (((0,), (0,)), ((), ())), preferred_element_type=jnp.float32
    )
    second_term = lax.dot_general(
        full_cotangent, hidden, (((0,), (0,)), ((), ())), preferred_element_type=jnp.float32
    )
    partial_sum = lax.psum_scatter(
        jnp.concatenate([first_term, second_term], axis=1), "row", scatter_dimension=0, tiled=True
    )
    summed = lax.psum(partial_sum, "dp")
    replica_weight = (lax.axis_index("dp") == 0).astype(jnp.float32)
    grad_in = summed[:, :local_units]
    grad_out_t = summed[:, local_units:]
    col_index = lax.axis_index("col")
    in_squared = grad_in * grad_in
    out_squared = grad_out_t * grad_out_t
    across_units = jnp.stack([jnp.sum(in_squared, axis=1), jnp.sum(out_squared, axis=1)])
    across_rows = (
        jnp.stack([jnp.sum(in_squared, axis=0), jnp.sum(out_squared, axis=0)]) * replica_weight
    )
    in_mask = jnp.where(col_index == 0, replica_weight, jnp.float32(0.0))
    out_mask = (lax.axis_index(("dp", "row")) == 0).astype(jnp.float32)
    unit_sums = lax.psum(across_units, "col")
    row_sums = lax.psum(across_rows, ("dp", "row"))
    in_row_new = moment_mix(in_row_moment, unit_sums[0], hidden_units)
    out_col_new = moment_mix(out_col_moment, unit_sums[1], hidden_units)
    in_col_new = moment_mix(in_col_moment, row_sums[0], model_width)
    out_row_new = moment_mix(out_row_moment, row_sums[1], model_width)
    mean_parts = jnp.stack([jnp.sum(in_row_new) * in_mask, jnp.sum(out_row_new) * out_mask])
    mean_totals = lax.psum(mean_parts, ("dp", "row", "col"))
    in_mean = mean_totals[0] / model_width
    out_mean = mean_totals[1] / hidden_units
    in_raw = grad_in / jnp.sqrt(in_row_new[:, None] * in_col_new[None, :] / in_mean)
    out_raw = grad_out_t / jnp.sqrt(out_col_new[:, None] * out_row_new[None, :] / out_mean)
    clip_parts = jnp.stack([jnp.sum(in_raw * in_raw), jnp.sum(out_raw * out_raw)]) * replica_weight
    clip_totals = lax.psum(clip_parts, ("dp", "row", "col"))
    entry_count = model_width * hidden_units
    in_rms = jnp.sqrt(clip_totals[0] / entry_count)
    out_rms = jnp.sqrt(clip_totals[1] / entry_count)
    in_update = in_raw / jnp.maximum(1.0, in_rms / CLIP_LIMIT)
    out_update_t = out_raw / jnp.maximum(1.0, out_rms / CLIP_LIMIT)
    return (input_grad, in_update, out_update_t.T, in_row_new, in_col_new, out_row_new, out_col_new)


def solution(mesh):
    placed = (
        P(("dp", "row"), "col"),
        P(("dp", "row"), "col"),
        P("row", "col"),
        P("col", "row"),
        P("row"),
        P("col"),
        P("col"),
        P("row"),
    )
    return jax.shard_map(
        local,
        mesh=mesh,
        in_specs=placed,
        out_specs=(
            P(("dp", "row"), "col"),
            P("row", "col"),
            P("col", "row"),
            P("row"),
            P("col"),
            P("col"),
            P("row"),
        ),
        check_vma=False,
    )
```

profile of v0, /device:TPU:1, one launch (start us, length us, event | category | flops | bytes accessed | tf_op | source)
XLA Modules:
  0.0 835.5 jit_solution(11522489711522134386)
XLA Ops:
  10.0 45.1 %all-gather.9.cloned.1.call-done = bf16[384,2048]{1,0:T(8,128)(2,1)} async-done(((bf16[384,512]{1,0:T(8,128)(2,1)}), bf16[384,2048]{1,0:T(8,128)(2,1)}) %all-gather.9.cloned.1.call-update) | async-done | bytes 1572880 | tf_op jit(solution)/shard_map/all_gather | solution.py:38
  55.1 53.8 %all-gather.11.cloned.1.call-done = bf16[2048,1024]{1,0:T(8,128)(2,1)} async-done(((bf16[64,1024]{1,0:T(8,128)(2,1)}), bf16[2048,1024]{1,0:T(8,128)(2,1)}) %all-gather.11.cloned.1.call-update) | async-done | bytes 4194320 | tf_op jit(solution)/shard_map/all_gather | solution.py:42
  108.8 4.4 fusion.27
  113.3 37.8 %all-gather.5.cloned.1.call-done = bf16[384,2048]{1,0:T(8,128)(2,1)} async-done(((bf16[384,512]{1,0:T(8,128)(2,1)}), bf16[384,2048]{1,0:T(8,128)(2,1)}) %all-gather.5.cloned.1.call-update) | async-done | bytes 1572880 | tf_op jit(solution)/shard_map/all_gather | solution.py:39
  151.2 7.3 convolution_bitcast_fusion
  158.4 46.3 %all-gather.7.cloned.1.call-done = bf16[1024,2048]{0,1:T(8,128)(2,1)} async-done(((bf16[1024,64]{0,1:T(8,128)(2,1)}), bf16[1024,2048]{0,1:T(8,128)(2,1)}) %all-gather.7.cloned.1.call-update) | async-done | bytes 4194320 | tf_op jit(solution)/shard_map/all_gather | solution.py:43
  204.8 5.1 fusion.6
  209.9 0.9 copy-done.5
  210.8 2.4 convolution_bitcast_fusion.1
  213.2 1.0 copy-done
  214.1 6.2 pad_maximum_fusion
  220.4 17.6 %copy.19 = f32[2048,2048]{1,0:T(8,128)} copy(f32[2048,2048]{0,1:T(8,128)} %pad_maximum_fusion) | data formatting | bytes 33554432
  238.0 120.9 %reduce-scatter.7.cloned.1.call-done = f32[64,2048]{1,0:T(8,128)} async-done(((f32[2048,2048]{1,0:T(8,128)}), f32[64,2048]{1,0:T(8,128)}) %reduce-scatter.7.cloned.1.call-update) | async-done | bytes 524304
  358.9 2.4 copy.20
  361.4 5.7 fusion.28
  367.1 73.1 %all-reduce.2.cloned.1.call-done = f32[64,2048]{0,1:T(8,128)} async-done(((f32[64,2048]{0,1:T(8,128)}), f32[64,2048]{0,1:T(8,128)}) %all-reduce.2.cloned.1.call-update) | async-done | bytes 524304 | tf_op jit(solution)/shard_map/psum | solution.py:73
  440.2 1.6 fusion.12
  441.9 205.9 %psum.37 = f32[2,1024]{1,0:T(2,128)S(1)} all-reduce(f32[2,1024]{1,0:T(2,128)S(1)} %maximum_multiply_fusion), channel_id=1, replica_groups=mesh['dp'=2,'row'=32,'col'=4] {'dp','row'}, use_global_device_ids=true, to_apply=%region_8.9 | all-reduce | flops 2048 | bytes 16384 | tf_op jit(solution)/shard_map/psum | solution.py:87
  649.1 7.6 psum.36
  658.1 86.9 %psum.38 = f32[2]{0:T(128)S(1)} all-reduce(f32[2]{0:T(128)S(1)} %pad_maximum_fusion.2), channel_id=1, replica_groups=mesh['dp'=2,'row'=32,'col'=4] {'dp','row','col'}, use_global_device_ids=true, to_apply=%region_11.12 | all-reduce | flops 2 | bytes 16 | tf_op jit(solution)/shard_map/psum | solution.py:93
  746.8 1.0 multiply_reduce_fusion.1
  747.8 1.3 maximum_multiply_fusion.1
  749.1 1.9 convert_element_type.14
  751.0 73.5 %psum.39 = f32[2]{0:T(128)S(1)} all-reduce(f32[2]{0:T(128)S(1)} %maximum_multiply_fusion.1), channel_id=1, replica_groups=mesh['dp'=2,'row'=32,'col'=4] {'dp','row','col'}, use_global_device_ids=true, to_apply=%region_14.15 | all-reduce | flops 2 | bytes 16 | tf_op jit(solution)/shard_map/psum | solution.py:99
  (54 shorter events, 7.7 us)
Async XLA Ops:
  7.2 47.9 %all-gather.9.cloned.1.call-start = ((), (), s32[]{:S(2)}) async-start(), calls=%async_computation.4 | async-start | bytes 1966080 | tf_op jit(solution)/shard_map/all_gather | solution.py:38
  7.9 100.9 %all-gather.11.cloned.1.call-start = ((), (), s32[]{:S(2)}) async-start(), calls=%async_computation.5 | async-start | bytes 4325376 | tf_op jit(solution)/shard_map/all_gather | solution.py:42
  8.6 142.5 %all-gather.5.cloned.1.call-start = ((), (), s32[]{:S(2)}) async-start(), calls=%async_computation.2 | async-start | bytes 1966080 | tf_op jit(solution)/shard_map/all_gather | solution.py:39
  9.4 195.4 %all-gather.7.cloned.1.call-start = ((), (), s32[]{:S(2)}) async-start(), calls=%async_computation.3 | async-start | bytes 4325376 | tf_op jit(solution)/shard_map/all_gather | solution.py:43
  10.0 348.9 %reduce-scatter.7.cloned.1.call-start = ((), (), s32[]{:S(2)}) async-start(), calls=%async_computation.8 | async-start | bytes 17301504
  113.3 37.9 %copy-start.4 = (f32[384,1024]{1,0:T(8,128)}, f32[384,1024]{1,0:T(8,128)S(1)}, u32[]{:S(2)}) copy-start(f32[384,1024]{1,0:T(8,128)S(1)} %fusion.27) | copy-start | bytes 4718596
  151.2 53.6 %copy-start.3 = (bf16[384,2048]{1,0:T(8,128)(2,1)S(1)}, bf16[384,2048]{1,0:T(8,128)(2,1)}, u32[]{:S(2)}) copy-start(bf16[384,2048]{1,0:T(8,128)(2,1)} %all-gather.5.cloned.1.call-done) | copy-start | bytes 4718596
  158.4 52.3 %copy-start.2 = (bf16[384,2048]{1,0:T(8,128)(2,1)S(1)}, bf16[384,2048]{1,0:T(8,128)(2,1)}, u32[]{:S(2)}) copy-start(bf16[384,2048]{1,0:T(8,128)(2,1)} %all-gather.9.cloned.1.call-done) | copy-start | bytes 4718596
  209.9 0.9 copy-start.5
  210.8 3.4 copy-start
  238.0 123.4 %copy-start.6 = (bf16[384,1024]{1,0:T(8,128)(2,1)S(1)}, bf16[384,1024]{1,0:T(8,128)(2,1)}, u32[]{:S(2)}) copy-start(bf16[384,1024]{1,0:T(8,128)(2,1)} %copy-done.5) | copy-start | bytes 2359300
  238.0 202.2 %all-reduce.2.cloned.1.call-start = ((), (), s32[]{:S(2)}) async-start(), calls=%async_computation.7 | async-start | bytes 2097152 | tf_op jit(solution)/shard_map/psum | solution.py:73
  361.3 387.8 %reduce-scatter.5.cloned.1.call-start = ((), (), s32[]{:S(2)}) async-start(), calls=%async_computation.6 | async-start | bytes 3932160 | tf_op jit(solution)/shard_map/reduce_scatter | solution.py:58
  367.0 280.8 %copy-start.11 = (f32[1024]{0:T(1024)S(1)}, f32[1024]{0:T(1024)}, u32[]{:S(2)}) copy-start(f32[1024]{0:T(1024)} %param.14) | copy-start | bytes 12292
  367.0 280.8 %copy-start.12 = (f32[1024]{0:T(1024)S(1)}, f32[1024]{0:T(1024)}, u32[]{:S(2)}) copy-start(f32[1024]{0:T(1024)} %param.13) | copy-start | bytes 12292
  367.0 289.7 %copy-start.13 = (f32[64]{0:T(128)S(1)}, f32[64]{0:T(128)}, u32[]{:S(2)}) copy-start(f32[64]{0:T(128)} %param.12) | copy-start | bytes 772
  367.0 289.7 %copy-start.14 = (f32[64]{0:T(128)S(1)}, f32[64]{0:T(128)}, u32[]{:S(2)}) copy-start(f32[64]{0:T(128)} %param.15) | copy-start | bytes 772
  440.2 306.6 %copy-start.1 = (f32[64,2048]{0,1:T(8,128)S(1)}, f32[64,2048]{0,1:T(8,128)}, u32[]{:S(2)}) copy-start(f32[64,2048]{0,1:T(8,128)} %all-reduce.2.cloned.1.call-done) | copy-start | bytes 1572868
  648.4 178.4 %copy-start.7 = (f32[1024]{0:T(1024)}, f32[1024]{0:T(1024)S(1)}, u32[]{:S(2)}) copy-start(f32[1024]{0:T(1024)S(1)} %get-tuple-element.30) | copy-start | bytes 12292
  648.4 178.4 %copy-start.8 = (f32[1024]{0:T(1024)}, f32[1024]{0:T(1024)S(1)}, u32[]{:S(2)}) copy-start(f32[1024]{0:T(1024)S(1)} %get-tuple-element.40) | copy-start | bytes 12292
  657.3 169.5 %copy-start.9 = (f32[64]{0:T(128)}, f32[64]{0:T(128)S(1)}, u32[]{:S(2)}) copy-start(f32[64]{0:T(128)S(1)} %get-tuple-element.28) | copy-start | bytes 772
  657.3 169.5 %copy-start.10 = (f32[64]{0:T(128)}, f32[64]{0:T(128)S(1)}, u32[]{:S(2)}) copy-start(f32[64]{0:T(128)S(1)} %get-tuple-element.35) | copy-start | bytes 772
Sparse Core Ops, SparseCore 0:
  9.8 45.2 all-gather.8
  57.6 51.1 all-gather.10
  110.7 40.4 all-gather.4
  153.6 51.1 all-gather.6
  238.1 120.7 reduce-scatter.6
  361.4 78.7 all-reduce.1
  442.9 63.0 reduce-scatter.4
where the time goes:
time: 836 us
  waiting for transfers between devices  380 us (45%)
  blocking collectives  374 us (45%)
  matrix products  24.9 us (3%)
  local copies, waits for them, and re-layouts  24.9 us (3%)
  between operations  18.3 us (2%)
  other arithmetic  13.7 us (2%)
    psum x1, blocking collectives, local(): row_sums = lax.psum(across_rows, ('dp', 'row'))  206 us
    unnamed x8, waiting for transfers between devices  123 us
    psum x1, blocking collectives, local(): mean_totals = lax.psum(mean_parts, ('dp', 'row', 'col'))  86.9 us
    psum x1, blocking collectives, local(): clip_totals = lax.psum(clip_parts, ('dp', 'row', 'col'))  73.5 us
    psum x1, waiting for transfers between devices, local(): summed = lax.psum(partial_sum, 'dp')  73.1 us
    all_gather x1, waiting for transfers between devices, local(): lax.all_gather(weight_in, 'row', axis=0, tiled=True)  53.8 us
    all_gather x1, waiting for transfers between devices, local(): lax.all_gather(weight_out, 'row', axis=1, tiled=True)  46.3 us
    all_gather x1, waiting for transfers between devices, local(): lax.all_gather(saved_input, 'col', axis=1, tiled=True)  45.1 us
  transfers between devices with their start and end apart: 7, of which 6 were waited for; matrix products, arithmetic and copies ran while one was open for 3% of the time, Pallas kernels for 0%

commit v1 on v0

v1 whole, which is shorter than its diff:
```python
import jax
import jax.numpy as jnp
from jax import lax
from jax.experimental import pallas as pl
from jax.experimental.pallas import tpu as pltpu
from jax.sharding import PartitionSpec as P

MESH = pl.DeviceIdType.MESH
F32 = jnp.float32
BF16 = jnp.bfloat16

GELU_SCALE = 0.7978845608028654
GELU_CUBIC = 0.044715
MOMENT_DECAY = 0.8
CLIP_LIMIT = 1.0
EPSILON_SQ = 1e-30

TOK, WIDTH, UNITS, BLK = 384, 2048, 1024, 512
ALL_UNITS = 4096
ENTRIES = WIDTH * ALL_UNITS

CORE_G, STAGE1, STAGE2, DP, SUMS, SWAP, MOM = 0, 8, 20, 32, 40, 80, 82
W_SWAP, W_RING1, W_RING2, W_PART, LINE, BACK = 83, 85, 89, 105, 121, 145
N_SEM = 157
CHUNKS = ((0, 256), (256, 128), (0, 384))


def gelu_parts(values):
    inner = GELU_SCALE * (values + GELU_CUBIC * values * values * values)
    tangent = jnp.tanh(inner)
    output = 0.5 * values * (1.0 + tangent)
    slope = 0.5 * (1.0 + tangent) + 0.5 * values * (1.0 - tangent * tangent) * GELU_SCALE * (
        1.0 + 3.0 * GELU_CUBIC * values * values
    )
    return (output, slope)


def kernel(
    x_ref, cot_ref, win_ref, wout_ref, in_row_ref, in_col_ref, out_row_ref, out_col_ref,
    ig_ref, in_upd_ref, out_upd_ref, in_row_out, in_col_out, out_row_out, out_col_out,
    dmom_ref, full, w_ref, acc, tr, act, g_own, g_send, g_recv, s1, r1, s2, r2, dp_s, dp_z, dp_r, dmom_in,
    za, xa, zb, xb, ratio, swap_u, swap_v, back_s, back_r, it_own, ig_s,
    ss, rs, local,
):
    d = lax.axis_index("dp")
    r = lax.axis_index("row")
    c = lax.axis_index("col")
    core = lax.rem(r, 2)
    x = lax.rem(r // 2, 4)
    y = r // 8
    p1 = x + core * (y - x)
    p2 = y + core * (x - y)
    k1, k2 = 2 + 6 * core, 8 - 6 * core
    t1, t2 = 1 + 3 * core, 4 - 3 * core
    m = core
    other = 1 - core

    def ring(position, step):
        return lax.rem(position + step, 4)

    def rowdev(q1, q2):
        return {"row": q1 * k1 + q2 * k2 + core}

    partner = {"row": r + 1 - 2 * core}
    right1, left1 = rowdev(ring(p1, 1), p2), rowdev(ring(p1, 3), p2)
    right2, left2 = rowdev(p1, ring(p2, 1)), rowdev(p1, ring(p2, 3))
    up2 = {"dp": lax.rem(d + c // 2, 2), "col": ring(c, 2)}
    down2 = {"dp": lax.rem(d + 1 - c // 2, 2), "col": ring(c, 2)}

    chip = y * 4 + x

    def along_xy(k):
        return {"row": lax.rem(chip + k, 16) * 2 + core}

    def along_z(k):
        return {"col": ring(c, k)}

    def along_z_and_cores(k):
        place = lax.rem(core * 4 + c + k, 8)
        return {"row": r - core + place // 4, "col": lax.rem(place, 4)}

    barrier = pltpu.get_barrier_semaphore()
    peers = [{"dp": 1 - d, "col": ring(c, 2)}]
    peers += [along_z_and_cores(k) for k in range(1, 8)]
    peers += [along_xy(k) for k in range(1, 16)]
    for peer in peers:
        pl.semaphore_signal(barrier, inc=1, device_id=peer, device_id_type=MESH)

    def chip_rows(q1, q2):
        return pl.ds(pl.multiple_of((q1 * t1 + q2 * t2) * 128, 128), 128)

    def half_rows(q1, q2, h):
        return pl.ds(pl.multiple_of((q1 * t1 + q2 * t2) * 128 + h * 64, 64), 64)

    own_rows = half_rows(p1, p2, core)
    loads = [
        pltpu.make_async_copy(x_ref, full.at[0, c], local.at[0]),
        pltpu.make_async_copy(cot_ref, full.at[1, c], local.at[1]),
        pltpu.make_async_copy(win_ref, w_ref.at[0, own_rows, :], local.at[2]),
        pltpu.make_async_copy(wout_ref, w_ref.at[1, own_rows, :], local.at[3]),
    ]
    for copy in loads:
        copy.start()
    for i, ref in enumerate((in_row_ref, out_col_ref)):
        dmom_ref[i] = jnp.broadcast_to(jnp.concatenate([ref[...], ref[...]], axis=1), (8, 128))

    for copy in loads:
        copy.wait()
    pl.semaphore_wait(barrier, len(peers))

    def send(src, dst, number, device):
        copy = pltpu.make_async_remote_copy(
            src_ref=src, dst_ref=dst, send_sem=ss.at[number], recv_sem=rs.at[number],
            device_id=device, device_id_type=MESH,
        )
        copy.start()
        return copy

    pending = []

    def start(src, dst, number, device):
        copy = send(src, dst, number, device)
        pending.append(copy)
        return copy

    def arrived(dst, number):
        pltpu.make_async_remote_copy(
            src_ref=dst, dst_ref=dst, send_sem=ss.at[number], recv_sem=rs.at[number],
            device_id=partner, device_id_type=MESH,
        ).wait_recv()

    def line_number(leftward, k, i, j):
        return LINE + ((leftward * 3 + k - 1) * 2 + j) * 2 + i

    def line_copy(leftward, k, i, j):
        rows = pl.ds(*CHUNKS[j])
        owner = c + (k - 1) if leftward else c - (k - 1)
        number = line_number(leftward, k, i, j)
        return pltpu.make_async_remote_copy(
            src_ref=full.at[i, owner, rows, :], dst_ref=full.at[i, owner, rows, :], send_sem=ss.at[number], recv_sem=rs.at[number],
            device_id={"col": ring(c, 3 if leftward else 1)}, device_id_type=MESH,
        )

    def line_sends(leftward, k):
        return (c > 0) & (c + (k - 1) <= 3) if leftward else (c < 3) & (c - (k - 1) >= 0)

    def line_gets(leftward, k):
        return c + k <= 3 if leftward else c - k >= 0

    def line_start(k, j):
        for leftward in (0, 1):
            @pl.when(line_sends(leftward, k))
            def _(leftward=leftward):
                for i in range(2):
                    line_copy(leftward, k, i, j).start()

    def hand_on(k, j, here=None):
        for i in range(2):
            for leftward in (0, 1):
                gets, sends = line_gets(leftward, k), line_sends(leftward, k + 1)
                if here is not None:
                    gets, sends = gets & here, sends & here

                @pl.when(gets)
                def _(i=i, leftward=leftward):
                    owner = c + k if leftward else c - k
                    arrived(full.at[i, owner, pl.ds(*CHUNKS[j]), :], line_number(leftward, k, i, j))

                if k < 3:
                    @pl.when(sends)
                    def _(i=i, leftward=leftward):
                        line_copy(leftward, k + 1, i, j).start()

    at_an_end = (c == 0) | (c == 3)
    inside = (c == 1) | (c == 2)
    line_start(1, 0)

    swaps = [start(w_ref.at[i, own_rows, :], w_ref.at[i, own_rows, :], W_SWAP + i, partner) for i in range(2)]
    mom = start(dmom_ref.at[other], dmom_in, MOM, partner)
    def weight_copy(q1, q2, number, device):
        block = w_ref.at[m, chip_rows(q1, q2), :]
        return start(block, block, number, device)

    def half_copy(q1, q2, h, number, device):
        block = w_ref.at[m, half_rows(q1, q2, h), :]
        return start(block, block, number, device)

    def second_ring(e):
        q1 = ring(p1, e)
        weight_copy(q1, p2, W_RING2 + e, right2)
        weight_copy(q1, p2, W_RING2 + 4 + e, left2)

    def second_ring_on(e):
        q1 = ring(p1, e)
        arrived(w_ref.at[m, chip_rows(q1, ring(p2, 3)), :], W_RING2 + e)
        half_copy(q1, ring(p2, 3), 0, W_RING2 + 8 + e, right2)
        arrived(w_ref.at[m, chip_rows(q1, ring(p2, 1)), :], W_RING2 + 4 + e)
        half_copy(q1, ring(p2, 1), 1, W_RING2 + 12 + e, left2)
        to_partner(e, 3)
        to_partner(e, 1)

    def to_partner(e, f):
        weight_copy(ring(p1, e), ring(p2, f), W_PART + 4 * e + f, partner)

    for i in range(2):
        swaps[i].wait_recv()
    weight_copy(p1, p2, W_RING1, right1)
    weight_copy(p1, p2, W_RING1 + 1, left1)
    second_ring(0)

    def transposed(b, j):
        first, count = CHUNKS[j]
        for i in range(2):
            for n in range(4):
                tr[i, b * 4 + n, :, first:first + count] = full[i, b, first:first + count, n * 128:(n + 1) * 128].T

    transposed(c, 0)
    arrived(w_ref.at[m, chip_rows(ring(p1, 3), p2), :], W_RING1)
    half_copy(ring(p1, 3), p2, 0, W_RING1 + 2, right1)
    arrived(w_ref.at[m, chip_rows(ring(p1, 1), p2), :], W_RING1 + 1)
    half_copy(ring(p1, 1), p2, 1, W_RING1 + 3, left1)
    second_ring(3)
    second_ring(1)
    to_partner(3, 0)
    to_partner(1, 0)
    second_ring_on(0)
    line_start(1, 1)
    hand_on(1, 0)
    for h in range(2):
        arrived(w_ref.at[m, half_rows(ring(p1, 2), p2, h), :], W_RING1 + 2 + h)
    second_ring(2)
    to_partner(2, 0)
    transposed(c, 1)
    second_ring_on(3)
    second_ring_on(1)
    second_ring_on(2)

    def both_sides(k, j, *work):
        for owner, there in ((c - k, c - k >= 0), (c + k, c + k <= 3)):
            @pl.when(there)
            def _(owner=owner):
                for part in work:
                    part(owner, j)

    hand_on(2, 0)
    both_sides(1, 0, transposed)
    for e in (0, 3, 1, 2):
        for h in range(2):
            arrived(w_ref.at[m, half_rows(ring(p1, e), ring(p2, 2), h), :], W_RING2 + 8 + 4 * h + e)
        to_partner(e, 2)

    def products(b, j, first=False):
        part = pl.ds(pl.multiple_of(b * BLK, BLK), BLK)
        rows = pl.ds(*CHUNKS[j])

        @pl.loop(0, 4)
        def _(n):
            cols = pl.ds(pl.multiple_of(n * 256, 256), 256)
            for i in range(2):
                value = jnp.dot(full[i, b, rows, :], w_ref[i, part, cols], preferred_element_type=F32)
                if first:
                    acc[i, rows, cols] = value
                else:
                    acc[i, rows, cols] += value

    def activate(j):
        rows = pl.ds(*CHUNKS[j])

        @pl.loop(0, 4)
        def _(n):
            cols = pl.ds(pl.multiple_of(n * 256, 256), 256)
            output, slope = gelu_parts(acc[0, rows, cols])
            act[1, rows, cols] = output.astype(BF16)
            act[0, rows, cols] = (acc[1, rows, cols] * slope).astype(BF16)

    def terms(t, j, store):
        rows = pl.ds(*CHUNKS[j])

        @pl.loop(0, 2)
        def _(n):
            inner = pl.ds(pl.multiple_of(n * 256, 256), 256)
            part = pl.ds(pl.multiple_of(t * BLK + n * 256, 256), 256)
            store(inner, lax.dot_general(
                act[0, rows, :], w_ref[0, part, :], (((1,), (1,)), ((), ())), preferred_element_type=F32))

    def back_copy(leftward, k, j):
        rows = pl.ds(*CHUNKS[j])
        number = BACK + (leftward * 3 + k - 1) * 2 + j
        return pltpu.make_async_remote_copy(
            src_ref=back_s.at[leftward, k - 1, rows, :], dst_ref=back_r.at[leftward, k - 1, rows, :],
            send_sem=ss.at[number], recv_sem=rs.at[number],
            device_id={"col": ring(c, 3 if leftward else 1)}, device_id_type=MESH,
        )

    def back_arrived(leftward, k, j):
        arrived(back_r.at[leftward, k, pl.ds(*CHUNKS[j]), :], BACK + (leftward * 3 + k) * 2 + j)

    def back_first(k, j):
        rows = pl.ds(*CHUNKS[j])
        for leftward in (0, 1):
            @pl.when(c == (3 if leftward else 0))
            def _(leftward=leftward):
                def keep(inner, value):
                    back_s[leftward, k - 1, rows, inner] = value.astype(BF16)

                terms(c - k if leftward else c + k, j, keep)
                back_copy(leftward, k, j).start()

    def back_on(k, j):
        rows = pl.ds(*CHUNKS[j])
        for leftward in (0, 1):
            sends = (c < 3) & (c - k >= 0) if leftward else (c > 0) & (c + k <= 3)

            @pl.when(sends)
            def _(leftward=leftward):
                back_arrived(leftward, k, j)

                def keep(inner, value):
                    back_s[leftward, k - 1, rows, inner] = (
                        value + back_r[leftward, k, rows, inner].astype(F32)).astype(BF16)

                terms(c - k if leftward else c + k, j, keep)
                back_copy(leftward, k, j).start()

    hand_on(1, 1)
    for e in range(4):
        for f in range(4):
            if e or f:
                there = pl.ds(pl.multiple_of((ring(p2, e) * t2 + ring(p1, f) * t1) * 128, 128), 128)
                arrived(w_ref.at[other, there, :], W_PART + 4 * e + f)
    products(c, 2, first=True)
    both_sides(1, 1, transposed)
    both_sides(1, 2, products)
    hand_on(2, 1, inside)
    both_sides(2, 0, transposed, products)
    hand_on(3, 0)
    both_sides(3, 0, transposed, products)
    activate(0)
    for k in (3, 2, 1):
        back_first(k, 0)
    hand_on(2, 1, at_an_end)
    both_sides(2, 1, transposed, products)
    hand_on(3, 1)
    both_sides(3, 1, transposed, products)
    activate(1)

    offsets = (2, 1, 3, 0)

    def group_product(matrix, chips, piece, store):
        lhs = jnp.concatenate([tr[matrix, chip] for chip in chips], axis=0)

        @pl.loop(2 * piece, 2 * piece + 2)
        def _(n):
            cols = pl.ds(pl.multiple_of(n * 256, 256), 256)
            store(n, jnp.dot(lhs, act[matrix, :, cols], preferred_element_type=F32))

    core_copies = {}

    def group(piece, g):
        theirs, mine = ring(p2, offsets[g]), ring(p1, offsets[g])

        def keep_sent(n, value):
            g_send[g, n] = value.astype(BF16)

        def keep_own(n, value):
            g_own[g, n] = value

        group_product(other, [theirs * t2 + q * t1 for q in range(4)], piece, keep_sent)
        pair = pl.ds(2 * piece, 2)
        core_copies[piece, g] = start(g_send.at[g, pair], g_recv.at[g, pair], CORE_G + 2 * g + piece, partner)
        group_product(m, [mine * t1 + q * t2 for q in range(4)], piece, keep_own)

    def reduced(dst, parts, rows):
        @pl.loop(0, rows // 128)
        def _(i):
            at = pl.ds(pl.multiple_of(i * 128, 128), 128)
            total = parts[0][at, :].astype(F32)
            for part in parts[1:]:
                total += part[at, :].astype(F32)
            dst[at, :] = total.astype(dst.dtype)

    ring1 = {}

    def chip_sum(g, n):
        return [g_own.at[g, n], g_recv.at[g, n]]

    def ring1_send(piece, g, h, which, device, extra=()):
        n = 2 * piece + h
        reduced(s1.at[g, n], chip_sum(g, n) + list(extra), BLK)
        ring1[piece, which] = start(s1.at[g, n], r1.at[which, piece], STAGE1 + 2 * which + piece, device)

    def first(piece):
        core_copies[piece, 0].wait_recv()
        ring1_send(piece, 0, 0, 0, right1)
        ring1_send(piece, 0, 1, 1, left1)

    def second(piece):
        core_copies[piece, 1].wait_recv()
        ring1_send(piece, 1, 1, 3, right1)
        core_copies[piece, 2].wait_recv()
        ring1_send(piece, 2, 0, 4, left1)

    def third(piece):
        ring1[piece, 0].wait_recv()
        ring1_send(piece, 1, 0, 2, right1, [r1.at[0, piece]])
        ring1[piece, 1].wait_recv()
        ring1_send(piece, 2, 1, 5, left1, [r1.at[1, piece]])

    ring2 = {}
    opp, nxt, prv = ring(p2, 2), ring(p2, 1), ring(p2, 3)

    def block(q, piece, h):
        at = pl.ds(pl.multiple_of(q * 128, 128), 128)
        return [
            ref.at[at, :] for ref in chip_sum(3, 2 * piece + h) + [r1.at[2 + h, piece], r1.at[4 + h, piece]]
        ]

    def ring2_send(piece, g, h, which, device, extra=()):
        n = 2 * piece + h
        reduced(s2.at[g, n], block((opp, nxt, prv)[g], piece, h) + list(extra), 128)
        ring2[piece, which] = start(s2.at[g, n], r2.at[which, piece], STAGE2 + 2 * which + piece, device)

    def ring2_first(piece):
        core_copies[piece, 3].wait_recv()
        for which in (3, 4, 2, 5):
            ring1[piece, which].wait_recv()
        ring2_send(piece, 0, 0, 0, right2)
        ring2_send(piece, 0, 1, 1, left2)
        ring2_send(piece, 1, 1, 3, right2)
        ring2_send(piece, 2, 0, 4, left2)

    def ring2_second(piece):
        ring2[piece, 0].wait_recv()
        ring2_send(piece, 1, 0, 2, right2, [r2.at[0, piece]])
        ring2[piece, 1].wait_recv()
        ring2_send(piece, 2, 1, 5, left2, [r2.at[1, piece]])

    travel = {}

    def dp_first(piece):
        for h, device in ((0, up2), (1, down2)):
            n = 2 * piece + h
            ring2[piece, 2 + h].wait_recv()
            ring2[piece, 4 + h].wait_recv()
            reduced(dp_s.at[n], block(p2, piece, h) + [r2.at[2 + h, piece], r2.at[4 + h, piece]], 128)
            travel[0, n] = start(dp_s.at[n], dp_z.at[n], DP + n, device)

    def dp_second(piece):
        for h, device in ((0, up2), (1, down2)):
            n = 2 * piece + h
            travel[0, n].wait_recv()
            travel[1, n] = start(dp_z.at[n], dp_r.at[n], DP + 4 + n, device)

    def keep_mine(first_row, count):
        def keep(inner, value):
            it_own[first_row:first_row + count, inner] = value
        return keep

    group(0, 0)
    group(0, 1)
    first(0)
    group(0, 2)
    second(0)
    group(1, 0)
    for k in (3, 2, 1):
        back_first(k, 1)
    third(0)
    group(1, 1)
    first(1)
    group(1, 2)
    second(1)
    group(0, 3)
    ring2_first(0)
    group(1, 3)
    third(1)
    ring2_second(0)
    back_on(2, 0)
    for j in range(2):
        terms(c, j, keep_mine(*CHUNKS[j]))
    ring2_first(1)
    dp_first(0)
    back_on(1, 0)
    ring2_second(1)
    back_on(2, 1)
    dp_second(0)
    dp_first(1)
    back_on(1, 1)
    dp_second(1)

    for leftward in (0, 1):
        @pl.when((c < 3) if leftward else (c > 0))
        def _(leftward=leftward):
            for j in range(2):
                back_arrived(leftward, 0, j)
            reduced(it_own, [it_own, back_r.at[leftward, 0]], TOK)

    reduced(ig_s, [it_own], TOK)
    ig_out = pltpu.make_async_copy(ig_s, ig_ref, local.at[4])
    ig_out.start()

    def across_start(place, number, count, device, value):
        place[...] = value
        return [start(place, place, number + k - 1, device(k)) for k in range(1, count + 1)]

    def added(values):
        while len(values) > 1:
            values = [values[i] + values[i + 1] for i in range(0, len(values), 2)]
        return values[0]

    def across_end(copies):
        for copy in copies:
            copy.wait_recv()

    mom.wait_recv()
    lane = lax.broadcasted_iota(jnp.int32, (8, 128), 1)
    old_d = jnp.where((lane // 64) == core, dmom_ref[m], dmom_in[...])[0:1, :]
    old_f = jnp.where(core == 0, in_col_ref[...], out_row_ref[...])
    old_f_sum = jnp.sum(old_f, axis=1, keepdims=True)
    old_d_sum = jnp.sum(old_d, axis=1, keepdims=True)
    col_sums = []
    lanes = None
    for n in range(4):
        travel[1, n].wait_recv()
        grad = dp_s[n].astype(F32) + dp_r[n].astype(F32)
        ratio[n] = grad
        squared = grad * grad
        col_sums.append(jnp.sum(squared, axis=0, keepdims=True))
        folded = squared[:, 0:128] + squared[:, 128:256]
        lanes = folded if n == 0 else lanes + folded
    sub = lax.broadcasted_iota(jnp.int32, (8, 256), 0)
    payload = jnp.where(sub == 4, old_d_sum, 0.0)
    for n in range(4):
        payload = jnp.where(sub == n, col_sums[n], payload)
    sent_xy = across_start(xa.at[chip], SUMS, 15, along_xy, payload)
    row_sums = jnp.sum(lanes.T, axis=0, keepdims=True)
    total = jnp.sum(row_sums, axis=1, keepdims=True)
    sub = lax.broadcasted_iota(jnp.int32, (8, 128), 0)
    sent_z = across_start(za.at[c], SUMS + 15, 3, along_z, jnp.where(sub == 0, row_sums, old_f_sum))
    across_end(sent_z)
    over_z = added([za[i] for i in range(4)])
    d_new = MOMENT_DECAY * old_d + (1.0 - MOMENT_DECAY) * (over_z[0:1, :] / ALL_UNITS + EPSILON_SQ)
    d_column = jnp.broadcast_to(1.0 / jnp.sqrt(d_new), (128, 128)).T[:, 0:1]
    across_end(sent_xy)
    over_xy = added([xa[i] for i in range(16)])
    old_mean = jnp.where(core == 0, over_xy[4:5, 0:1] / WIDTH, over_z[1:2, 0:1] / ALL_UNITS)
    f_new = [
        MOMENT_DECAY * old_f[:, n * 256:(n + 1) * 256]
        + (1.0 - MOMENT_DECAY) * (over_xy[n:n + 1, :] / WIDTH + EPSILON_SQ)
        for n in range(4)
    ]
    lanes = None
    for n in range(4):
        value = ratio[n] * (d_column * (1.0 / jnp.sqrt(f_new[n])))
        ratio[n] = value
        folded = value[:, 0:128] * value[:, 0:128] + value[:, 128:256] * value[:, 128:256]
        lanes = folded if n == 0 else lanes + folded
    folded = lanes[0:8]
    for i in range(1, 16):
        folded += lanes[i * 8:(i + 1) * 8]
    payload = jnp.concatenate([folded, jnp.where(sub == 0, total, old_mean)], axis=0)
    sent_z = across_start(zb.at[core, c], SUMS + 18, 7, along_z_and_cores, payload)

    theirs_at = pl.ds(pl.multiple_of(other * 64, 64), 64)
    swap_v[0] = jnp.zeros((8, UNITS), F32)
    for n in range(4):
        swap_u[0, :, n * 256:(n + 1) * 256] = ratio[n, theirs_at, :]
        swap_v[0, 0:1, n * 256:(n + 1) * 256] = f_new[n]
    swap_v[0, 1:2, 0:128] = d_new
    sent_u = start(swap_u.at[0], swap_u.at[1], SWAP, partner)
    sent_v = start(swap_v.at[0], swap_v.at[1], SWAP + 1, partner)

    across_end(sent_z)
    payload = jnp.stack([added([zb[i, j] for j in range(4)]) for i in range(2)])
    sent_xy = across_start(xb.at[chip], SUMS + 25, 15, along_xy, payload)
    across_end(sent_xy)
    factors = []
    for i in range(2):
        over_all = added([xb[j, i] for j in range(16)])
        mean = MOMENT_DECAY * (over_all[9:10, 0:1] / 64.0) + (1.0 - MOMENT_DECAY) * (
            over_all[8:9, 0:1] / ENTRIES + EPSILON_SQ)
        rms = jnp.sqrt(mean * (jnp.sum(over_all[0:8], keepdims=True) / ENTRIES))
        factors.append(jnp.sqrt(mean) / jnp.maximum(1.0, rms / CLIP_LIMIT))

    def own_lanes(value):
        return jnp.where(core == 0, value[:, 0:64], value[:, 64:128])

    sent_v.wait_recv()
    sent_u.wait_recv()

    def finish(update, row_of, d_out, f_out, which, scale):
        d_out[...] = own_lanes(swap_v[which, 1:2, 0:128])
        f_out[...] = swap_v[which, 0:1, :]
        for n in range(4):
            update[:, n * 256:(n + 1) * 256] = row_of(n) * scale

    def theirs(n):
        return swap_u[1, :, n * 256:(n + 1) * 256]

    @pl.when(core == 0)
    def _():
        finish(in_upd_ref, lambda n: ratio[n, 0:64, :], in_row_out, in_col_out, 0, factors[0])
        finish(out_upd_ref, theirs, out_col_out, out_row_out, 1, factors[1])

    @pl.when(core == 1)
    def _():
        finish(out_upd_ref, lambda n: ratio[n, 64:128, :], out_col_out, out_row_out, 0, factors[1])
        finish(in_upd_ref, theirs, in_row_out, in_col_out, 1, factors[0])

    ig_out.wait()
    for copy in pending:
        copy.wait_send()
    for leftward in (0, 1):
        for k in (1, 2, 3):
            @pl.when(line_sends(leftward, k))
            def _(leftward=leftward, k=k):
                for j in range(2):
                    for i in range(2):
                        line_copy(leftward, k, i, j).wait_send()

            @pl.when((c - k >= 0) if leftward else (c + k <= 3))
            def _(leftward=leftward, k=k):
                for j in range(2):
                    back_copy(leftward, k, j).wait_send()


def fused(*operands):
    vmem = pl.BlockSpec(memory_space=pltpu.VMEM)
    anywhere = pl.BlockSpec(memory_space=pl.ANY)
    return pl.pallas_call(
        kernel,
        out_shape=(
            jax.ShapeDtypeStruct((TOK, BLK), BF16),
            jax.ShapeDtypeStruct((64, UNITS), F32),
            jax.ShapeDtypeStruct((64, UNITS), F32),
            jax.ShapeDtypeStruct((1, 64), F32),
            jax.ShapeDtypeStruct((1, UNITS), F32),
            jax.ShapeDtypeStruct((1, UNITS), F32),
            jax.ShapeDtypeStruct((1, 64), F32),
        ),
        in_specs=[anywhere] * 4 + [vmem] * 4,
        out_specs=(anywhere,) + (vmem,) * 6,
        scratch_shapes=[
            pltpu.VMEM((2, 8, 128), F32),
            pltpu.VMEM((2, 4, TOK, BLK), BF16),
            pltpu.VMEM((2, WIDTH, UNITS), BF16),
            pltpu.VMEM((2, TOK, UNITS), F32),
            pltpu.VMEM((2, 16, 128, TOK), BF16),
            pltpu.VMEM((2, TOK, UNITS), BF16),
            pltpu.VMEM((4, 4, 512, 256), F32),
            pltpu.VMEM((4, 4, 512, 256), BF16),
            pltpu.VMEM((4, 4, 512, 256), BF16),
            pltpu.VMEM((3, 4, 512, 256), BF16),
            pltpu.VMEM((6, 2, 512, 256), BF16),
            pltpu.VMEM((3, 4, 128, 256), BF16),
            pltpu.VMEM((6, 2, 128, 256), BF16),
            pltpu.VMEM((4, 128, 256), BF16),
            pltpu.VMEM((4, 128, 256), BF16),
            pltpu.VMEM((4, 128, 256), BF16),
            pltpu.VMEM((8, 128), F32),
            pltpu.VMEM((4, 8, 128), F32),
            pltpu.VMEM((16, 8, 256), F32),
            pltpu.VMEM((2, 4, 16, 128), F32),
            pltpu.VMEM((16, 2, 16, 128), F32),
            pltpu.VMEM((4, 128, 256), F32),
            pltpu.VMEM((2, 64, UNITS), F32),
            pltpu.VMEM((2, 8, UNITS), F32),
            pltpu.VMEM((2, 3, TOK, BLK), BF16),
            pltpu.VMEM((2, 3, TOK, BLK), BF16),
            pltpu.VMEM((TOK, BLK), F32),
            pltpu.VMEM((TOK, BLK), BF16),
            pltpu.SemaphoreType.DMA((N_SEM,)),
            pltpu.SemaphoreType.DMA((N_SEM,)),
            pltpu.SemaphoreType.DMA((5,)),
        ],
        compiler_params=pltpu.CompilerParams(
            collective_id=0, has_side_effects=True, vmem_limit_bytes=60 * 1024 * 1024
        ),
        cost_estimate=pl.CostEstimate(
            flops=10 * TOK * WIDTH * UNITS, bytes_accessed=16 * 2**20, transcendentals=TOK * UNITS
        ),
    )(*operands)


def handed_out_kernel(*refs):
    count = len(refs) // 2
    for i in range(count):
        refs[count + i][...] = refs[i][...]


def handed_out(*results):
    vmem = pl.BlockSpec(memory_space=pltpu.VMEM)
    return pl.pallas_call(
        handed_out_kernel,
        out_shape=tuple(jax.ShapeDtypeStruct(result.shape, result.dtype) for result in results),
        in_specs=[vmem] * len(results),
        out_specs=(vmem,) * len(results),
        compiler_params=pltpu.CompilerParams(vmem_limit_bytes=60 * 1024 * 1024),
    )(*results)


def per_device(
    saved_input, cotangent, weight_in, weight_out, in_row_moment, in_col_moment, out_row_moment, out_col_moment
):
    input_grad, in_update, out_update_t, in_row, in_col, out_row, out_col = handed_out(*fused(
        saved_input, cotangent, weight_in, weight_out.T, in_row_moment.reshape(1, 64), in_col_moment.reshape(1, UNITS),
        out_row_moment.reshape(1, UNITS), out_col_moment.reshape(1, 64),
    ))
    return (
        input_grad, in_update, out_update_t.T, in_row.reshape(64), in_col.reshape(UNITS), out_row.reshape(UNITS),
        out_col.reshape(64),
    )


def solution(mesh):
    placed = (
        P(("dp", "row"), "col"), P(("dp", "row"), "col"), P("row", "col"), P("col", "row"),
        P("row"), P("col"), P("col"), P("row"),
    )
    return jax.shard_map(
        per_device,
        mesh=mesh,
        in_specs=placed,
        out_specs=(
            P(("dp", "row"), "col"), P("row", "col"), P("col", "row"), P("row"), P("col"), P("col"), P("row"),
        ),
        check_vma=False,
    )
```

time: 836 us -> 128 us (0.15)
  waiting for transfers between devices: 380 us -> 0 us
  blocking collectives: 374 us -> 0 us
  Pallas kernels: 0 us -> 127 us
  matrix products: 24.9 us -> 0 us
  local copies, waits for them, and re-layouts: 24.9 us -> 0 us
  between operations: 18.3 us -> 0.64 us
  other arithmetic: 13.7 us -> 0 us
    psum x4 -> x0, blocking collectives: 374 us -> none  [the longest x1 206 us: local(): row_sums = lax.psum(across_rows, ('dp', 'row'))]
    all_gather x4 -> x0, waiting for transfers between devices: 183 us -> none  [the longest x1 53.8 us: local(): lax.all_gather(weight_in, 'row', axis=0, tiled=True)]
    pallas_call x0 -> x2, Pallas kernels: none -> 127 us  [the longest x1 125 us: fused(): pl.pallas_call(kernel, out_shape=(jax.ShapeDtypeStruct((TOK, BLK), BF16),...]
    unnamed x8 -> x0, waiting for transfers between devices: 123 us -> none
    psum x1 -> x0, waiting for transfers between devices: 73.1 us -> none  [local(): summed = lax.psum(partial_sum, 'dp')]
    dot_general x5 -> x0, matrix products: 24.9 us -> none  [the longest x1 7.27 us: local(): lax.dot_general(full_cotangent, hidden, (((0,), (0,)), ((), ())), preferr...]
    unnamed x34 -> x0, local copies, waits for them, and re-layouts: 23.6 us -> none
  transfers between devices with their start and end apart: 7 -> 0, of which waited for: 6 -> 0; matrix products, arithmetic and copies ran while one was open for 3% -> 0% of each run, Pallas kernels for 0% -> 0%
where the time goes in v1:
time: 128 us
  Pallas kernels  127 us (99%)
    pallas_call x1, Pallas kernels, fused(): pl.pallas_call(kernel, out_shape=(jax.ShapeDtypeStruct((TOK, BLK), BF16),...  125 us

profile of v1, /device:TPU:1, one launch (start us, length us, event | category | flops | bytes accessed | tf_op | source)
XLA Modules:
  0.0 127.8 jit_solution(12124933617975355837)
XLA Ops:
  0.6 125.0 %shard_map.135 = (bf16[384,512]{1,0:T(8,128)(2,1)}, f32[64,1024]{1,0:T(8,128)}, f32[64,1024]{1,0:T(8,128)}, f32[1,64]{1,0:T(1,128)}, f32[1,1024]{1,0:T(1,128)}, /*index=5*/f32[1,1024]{1,0:T(1,128)}, f32[1,64]{1,0:T(1,128)}) custom-call(bf16[384,512]{1,0:T(8,128)(2,1)} %x_ref.1, bf16[384,512]{1,0:T(8,128)(2,1)} %cot_ref.1, bf16[64,1024]{1,0:T(8,128)(2,1)} %win_ref.1, ...), custom_call_target="tpu_custom_call" | custom-call | flops 8053063680 | bytes 16777216 | tf_op jit(solution)/shard_map/pallas_call | solution.py:629
  125.7 2.1 %shard_map.136 = (bf16[384,512]{1,0:T(8,128)(2,1)}, f32[64,1024]{1,0:T(8,128)}, f32[64,1024]{1,0:T(8,128)}, f32[1,64]{1,0:T(1,128)}, f32[1,1024]{1,0:T(1,128)}, /*index=5*/f32[1,1024]{1,0:T(1,128)}, f32[1,64]{1,0:T(1,128)}) custom-call(bf16[384,512]{1,0:T(8,128)(2,1)} %get-tuple-element.21.refs_0_, f32[64,1024]{1,0:T(8,128)} %get-tuple-element.22.refs_1_, ...), custom_call_target="tpu_custom_call" | custom-call | tf_op jit(solution)/shard_map/pallas_call | solution.py:692

commit v2 on v1

--- a/solution.py
+++ b/solution.py
@@ -36,9 +36,9 @@
 
 
 def kernel(
-    x_ref, cot_ref, win_ref, wout_ref, in_row_ref, in_col_ref, out_row_ref, out_col_ref,
+    x_ref, cot_ref, win_ref, wout_ref, in_row_hbm, in_col_hbm, out_row_hbm, out_col_hbm,
     ig_ref, in_upd_ref, out_upd_ref, in_row_out, in_col_out, out_row_out, out_col_out,
-    dmom_ref, full, w_ref, acc, tr, act, g_own, g_send, g_recv, s1, r1, s2, r2, dp_s, dp_z, dp_r, dmom_in,
+    in_row_ref, in_col_ref, out_row_ref, out_col_ref, dmom_ref, full, w_ref, acc, tr, act, g_own, g_send, g_recv, s1, r1, s2, r2, dp_s, dp_z, dp_r, dmom_in,
     za, xa, zb, xb, ratio, swap_u, swap_v, back_s, back_r, it_own, ig_s,
     ss, rs, local,
 ):
@@ -98,14 +98,17 @@
         pltpu.make_async_copy(cot_ref, full.at[1, c], local.at[1]),
         pltpu.make_async_copy(win_ref, w_ref.at[0, own_rows, :], local.at[2]),
         pltpu.make_async_copy(wout_ref, w_ref.at[1, own_rows, :], local.at[3]),
+        pltpu.make_async_copy(in_row_hbm, in_row_ref, local.at[5]),
+        pltpu.make_async_copy(in_col_hbm, in_col_ref, local.at[6]),
+        pltpu.make_async_copy(out_row_hbm, out_row_ref, local.at[7]),
+        pltpu.make_async_copy(out_col_hbm, out_col_ref, local.at[8]),
     ]
     for copy in loads:
         copy.start()
+    for copy in loads:
+        copy.wait()
     for i, ref in enumerate((in_row_ref, out_col_ref)):
         dmom_ref[i] = jnp.broadcast_to(jnp.concatenate([ref[...], ref[...]], axis=1), (8, 128))
-
-    for copy in loads:
-        copy.wait()
     pl.semaphore_wait(barrier, len(peers))
 
     def send(src, dst, number, device):
@@ -154,25 +157,19 @@
                 for i in range(2):
                     line_copy(leftward, k, i, j).start()
 
-    def hand_on(k, j, here=None):
+    def hand_on(k, j):
         for i in range(2):
             for leftward in (0, 1):
-                gets, sends = line_gets(leftward, k), line_sends(leftward, k + 1)
-                if here is not None:
-                    gets, sends = gets & here, sends & here
-
-                @pl.when(gets)
+                @pl.when(line_gets(leftward, k))
                 def _(i=i, leftward=leftward):
                     owner = c + k if leftward else c - k
                     arrived(full.at[i, owner, pl.ds(*CHUNKS[j]), :], line_number(leftward, k, i, j))
 
                 if k < 3:
-                    @pl.when(sends)
+                    @pl.when(line_sends(leftward, k + 1))
                     def _(i=i, leftward=leftward):
                         line_copy(leftward, k + 1, i, j).start()
 
-    at_an_end = (c == 0) | (c == 3)
-    inside = (c == 1) | (c == 2)
     line_start(1, 0)
 
     swaps = [start(w_ref.at[i, own_rows, :], w_ref.at[i, own_rows, :], W_SWAP + i, partner) for i in range(2)]
@@ -233,6 +230,7 @@
     transposed(c, 1)
     second_ring_on(3)
     second_ring_on(1)
+    hand_on(1, 1)
     second_ring_on(2)
 
     def both_sides(k, j, *work):
@@ -248,6 +246,8 @@
         for h in range(2):
             arrived(w_ref.at[m, half_rows(ring(p1, e), ring(p2, 2), h), :], W_RING2 + 8 + 4 * h + e)
         to_partner(e, 2)
+    both_sides(1, 1, transposed)
+    both_sides(2, 0, transposed)
 
     def products(b, j, first=False):
         part = pl.ds(pl.multiple_of(b * BLK, BLK), BLK)
@@ -283,6 +283,11 @@
             store(inner, lax.dot_general(
                 act[0, rows, :], w_ref[0, part, :], (((1,), (1,)), ((), ())), preferred_element_type=F32))
 
+    def keep_mine(first_row, count):
+        def keep(inner, value):
+            it_own[first_row:first_row + count, inner] = value
+        return keep
+
     def back_copy(leftward, k, j):
         rows = pl.ds(*CHUNKS[j])
         number = BACK + (leftward * 3 + k - 1) * 2 + j
@@ -322,27 +327,26 @@
                 terms(c - k if leftward else c + k, j, keep)
                 back_copy(leftward, k, j).start()
 
-    hand_on(1, 1)
     for e in range(4):
         for f in range(4):
             if e or f:
                 there = pl.ds(pl.multiple_of((ring(p2, e) * t2 + ring(p1, f) * t1) * 128, 128), 128)
                 arrived(w_ref.at[other, there, :], W_PART + 4 * e + f)
     products(c, 2, first=True)
-    both_sides(1, 1, transposed)
+    hand_on(2, 1)
     both_sides(1, 2, products)
-    hand_on(2, 1, inside)
-    both_sides(2, 0, transposed, products)
+    both_sides(2, 1, transposed)
+    both_sides(2, 2, products)
     hand_on(3, 0)
-    both_sides(3, 0, transposed, products)
+    both_sides(3, 0, products)
     activate(0)
     for k in (3, 2, 1):
         back_first(k, 0)
-    hand_on(2, 1, at_an_end)
-    both_sides(2, 1, transposed, products)
+    both_sides(3, 0, transposed)
     hand_on(3, 1)
-    both_sides(3, 1, transposed, products)
+    both_sides(3, 1, products)
     activate(1)
+    both_sides(3, 1, transposed)
 
     offsets = (2, 1, 3, 0)
 
@@ -356,18 +360,22 @@
 
     core_copies = {}
 
-    def group(piece, g):
-        theirs, mine = ring(p2, offsets[g]), ring(p1, offsets[g])
+    def group_theirs(piece, g):
+        theirs = ring(p2, offsets[g])
 
         def keep_sent(n, value):
             g_send[g, n] = value.astype(BF16)
-
-        def keep_own(n, value):
-            g_own[g, n] = value
 
         group_product(other, [theirs * t2 + q * t1 for q in range(4)], piece, keep_sent)
         pair = pl.ds(2 * piece, 2)
         core_copies[piece, g] = start(g_send.at[g, pair], g_recv.at[g, pair], CORE_G + 2 * g + piece, partner)
+
+    def group_own(piece, g):
+        mine = ring(p1, offsets[g])
+
+        def keep_own(n, value):
+            g_own[g, n] = value
+
         group_product(m, [mine * t1 + q * t2 for q in range(4)], piece, keep_own)
 
     def reduced(dst, parts, rows):
@@ -451,34 +459,36 @@
             travel[0, n].wait_recv()
             travel[1, n] = start(dp_z.at[n], dp_r.at[n], DP + 4 + n, device)
 
-    def keep_mine(first_row, count):
-        def keep(inner, value):
-            it_own[first_row:first_row + count, inner] = value
-        return keep
-
-    group(0, 0)
-    group(0, 1)
+    group_theirs(0, 0)
+    group_theirs(0, 1)
+    group_own(0, 0)
+    group_theirs(0, 2)
+    group_own(0, 1)
+    group_own(0, 2)
     first(0)
-    group(0, 2)
     second(0)
-    group(1, 0)
+    group_theirs(1, 0)
+    group_own(1, 0)
     for k in (3, 2, 1):
         back_first(k, 1)
     third(0)
-    group(1, 1)
+    group_theirs(1, 1)
+    group_own(1, 1)
     first(1)
-    group(1, 2)
+    group_theirs(1, 2)
+    group_own(1, 2)
     second(1)
-    group(0, 3)
+    group_theirs(0, 3)
+    group_own(0, 3)
     ring2_first(0)
-    group(1, 3)
+    group_theirs(1, 3)
+    group_own(1, 3)
     third(1)
     ring2_second(0)
     back_on(2, 0)
-    for j in range(2):
-        terms(c, j, keep_mine(*CHUNKS[j]))
+    terms(c, 2, keep_mine(*CHUNKS[2]))
+    dp_first(0)
     ring2_first(1)
-    dp_first(0)
     back_on(1, 0)
     ring2_second(1)
     back_on(2, 1)
@@ -637,9 +647,13 @@
             jax.ShapeDtypeStruct((1, UNITS), F32),
             jax.ShapeDtypeStruct((1, 64), F32),
         ),
-        in_specs=[anywhere] * 4 + [vmem] * 4,
+        in_specs=[anywhere] * 8,
         out_specs=(anywhere,) + (vmem,) * 6,
         scratch_shapes=[
+            pltpu.VMEM((1, 64), F32),
+            pltpu.VMEM((1, UNITS), F32),
+            pltpu.VMEM((1, UNITS), F32),
+            pltpu.VMEM((1, 64), F32),
             pltpu.VMEM((2, 8, 128), F32),
             pltpu.VMEM((2, 4, TOK, BLK), BF16),
             pltpu.VMEM((2, WIDTH, UNITS), BF16),
@@ -670,7 +684,7 @@
             pltpu.VMEM((TOK, BLK), BF16),
             pltpu.SemaphoreType.DMA((N_SEM,)),
             pltpu.SemaphoreType.DMA((N_SEM,)),
-            pltpu.SemaphoreType.DMA((5,)),
+            pltpu.SemaphoreType.DMA((9,)),
         ],
         compiler_params=pltpu.CompilerParams(
             collective_id=0, has_side_effects=True, vmem_limit_bytes=60 * 1024 * 1024

time: 128 us -> 127 us (level)
  no operation moved by 1% of the time
where the time goes in v2:
time: 127 us
  Pallas kernels  127 us (100%)
    pallas_call x1, Pallas kernels, fused(): pl.pallas_call(kernel, out_shape=(jax.ShapeDtypeStruct((TOK, BLK), BF16),...  124 us

profile of v2, /device:TPU:1, one launch (start us, length us, event | category | flops | bytes accessed | tf_op | source)
XLA Modules:
  0.0 127.2 jit_solution(2989781328483674932)
XLA Ops:
  0.6 124.4 %shard_map.135 = (bf16[384,512]{1,0:T(8,128)(2,1)}, f32[64,1024]{1,0:T(8,128)}, f32[64,1024]{1,0:T(8,128)}, f32[1,64]{1,0:T(1,128)}, f32[1,1024]{1,0:T(1,128)}, /*index=5*/f32[1,1024]{1,0:T(1,128)}, f32[1,64]{1,0:T(1,128)}) custom-call(bf16[384,512]{1,0:T(8,128)(2,1)} %x_ref.1, bf16[384,512]{1,0:T(8,128)(2,1)} %cot_ref.1, bf16[64,1024]{1,0:T(8,128)(2,1)} %win_ref.1, ...), custom_call_target="tpu_custom_call" | custom-call | flops 8053063680 | bytes 16777216 | tf_op jit(solution)/shard_map/pallas_call | solution.py:639
  125.0 2.1 %shard_map.136 = (bf16[384,512]{1,0:T(8,128)(2,1)}, f32[64,1024]{1,0:T(8,128)}, f32[64,1024]{1,0:T(8,128)}, f32[1,64]{1,0:T(1,128)}, f32[1,1024]{1,0:T(1,128)}, /*index=5*/f32[1,1024]{1,0:T(1,128)}, f32[1,64]{1,0:T(1,128)}) custom-call(bf16[384,512]{1,0:T(8,128)(2,1)} %get-tuple-element.21.refs_0_, f32[64,1024]{1,0:T(8,128)} %get-tuple-element.22.refs_1_, ...), custom_call_target="tpu_custom_call" | custom-call | tf_op jit(solution)/shard_map/pallas_call | solution.py:706

commit v3 on v2

--- a/solution.py
+++ b/solution.py
@@ -253,7 +253,7 @@
         part = pl.ds(pl.multiple_of(b * BLK, BLK), BLK)
         rows = pl.ds(*CHUNKS[j])
 
-        @pl.loop(0, 4)
+        @pl.loop(0, 4, unroll=2)
         def _(n):
             cols = pl.ds(pl.multiple_of(n * 256, 256), 256)
             for i in range(2):
@@ -276,7 +276,7 @@
     def terms(t, j, store):
         rows = pl.ds(*CHUNKS[j])
 
-        @pl.loop(0, 2)
+        @pl.loop(0, 2, unroll=True)
         def _(n):
             inner = pl.ds(pl.multiple_of(n * 256, 256), 256)
             part = pl.ds(pl.multiple_of(t * BLK + n * 256, 256), 256)
@@ -353,7 +353,7 @@
     def group_product(matrix, chips, piece, store):
         lhs = jnp.concatenate([tr[matrix, chip] for chip in chips], axis=0)
 
-        @pl.loop(2 * piece, 2 * piece + 2)
+        @pl.loop(2 * piece, 2 * piece + 2, unroll=True)
         def _(n):
             cols = pl.ds(pl.multiple_of(n * 256, 256), 256)
             store(n, jnp.dot(lhs, act[matrix, :, cols], preferred_element_type=F32))
@@ -379,7 +379,7 @@
         group_product(m, [mine * t1 + q * t2 for q in range(4)], piece, keep_own)
 
     def reduced(dst, parts, rows):
-        @pl.loop(0, rows // 128)
+        @pl.loop(0, rows // 128, unroll=True)
         def _(i):
             at = pl.ds(pl.multiple_of(i * 128, 128), 128)
             total = parts[0][at, :].astype(F32)

time: 127 us -> 126 us (level)
  Pallas kernels: 127 us -> 125 us
where the time goes in v3:
time: 126 us
  Pallas kernels  125 us (99%)
    pallas_call x1, Pallas kernels, fused(): pl.pallas_call(kernel, out_shape=(jax.ShapeDtypeStruct((TOK, BLK), BF16),...  123 us

profile of v3, /device:TPU:1, one launch (start us, length us, event | category | flops | bytes accessed | tf_op | source)
XLA Modules:
  0.0 125.9 jit_solution(1693430141901613769)
XLA Ops:
  0.6 123.2 %shard_map.135 = (bf16[384,512]{1,0:T(8,128)(2,1)}, f32[64,1024]{1,0:T(8,128)}, f32[64,1024]{1,0:T(8,128)}, f32[1,64]{1,0:T(1,128)}, f32[1,1024]{1,0:T(1,128)}, /*index=5*/f32[1,1024]{1,0:T(1,128)}, f32[1,64]{1,0:T(1,128)}) custom-call(bf16[384,512]{1,0:T(8,128)(2,1)} %x_ref.1, bf16[384,512]{1,0:T(8,128)(2,1)} %cot_ref.1, bf16[64,1024]{1,0:T(8,128)(2,1)} %win_ref.1, ...), custom_call_target="tpu_custom_call" | custom-call | flops 8053063680 | bytes 16777216 | tf_op jit(solution)/shard_map/pallas_call | solution.py:639
  123.8 2.1 %shard_map.136 = (bf16[384,512]{1,0:T(8,128)(2,1)}, f32[64,1024]{1,0:T(8,128)}, f32[64,1024]{1,0:T(8,128)}, f32[1,64]{1,0:T(1,128)}, f32[1,1024]{1,0:T(1,128)}, /*index=5*/f32[1,1024]{1,0:T(1,128)}, f32[1,64]{1,0:T(1,128)}) custom-call(bf16[384,512]{1,0:T(8,128)(2,1)} %get-tuple-element.21.refs_0_, f32[64,1024]{1,0:T(8,128)} %get-tuple-element.22.refs_1_, ...), custom_call_target="tpu_custom_call" | custom-call | tf_op jit(solution)/shard_map/pallas_call | solution.py:706

commit v4 on v3

--- a/solution.py
+++ b/solution.py
@@ -486,7 +486,6 @@
     third(1)
     ring2_second(0)
     back_on(2, 0)
-    terms(c, 2, keep_mine(*CHUNKS[2]))
     dp_first(0)
     ring2_first(1)
     back_on(1, 0)
@@ -496,17 +495,6 @@
     dp_first(1)
     back_on(1, 1)
     dp_second(1)
-
-    for leftward in (0, 1):
-        @pl.when((c < 3) if leftward else (c > 0))
-        def _(leftward=leftward):
-            for j in range(2):
-                back_arrived(leftward, 0, j)
-            reduced(it_own, [it_own, back_r.at[leftward, 0]], TOK)
-
-    reduced(ig_s, [it_own], TOK)
-    ig_out = pltpu.make_async_copy(ig_s, ig_ref, local.at[4])
-    ig_out.start()
 
     def across_start(place, number, count, device, value):
         place[...] = value
@@ -546,6 +534,7 @@
     total = jnp.sum(row_sums, axis=1, keepdims=True)
     sub = lax.broadcasted_iota(jnp.int32, (8, 128), 0)
     sent_z = across_start(za.at[c], SUMS + 15, 3, along_z, jnp.where(sub == 0, row_sums, old_f_sum))
+    terms(c, 2, keep_mine(*CHUNKS[2]))
     across_end(sent_z)
     over_z = added([za[i] for i in range(4)])
     d_new = MOMENT_DECAY * old_d + (1.0 - MOMENT_DECAY) * (over_z[0:1, :] / ALL_UNITS + EPSILON_SQ)
@@ -578,6 +567,17 @@
     swap_v[0, 1:2, 0:128] = d_new
     sent_u = start(swap_u.at[0], swap_u.at[1], SWAP, partner)
     sent_v = start(swap_v.at[0], swap_v.at[1], SWAP + 1, partner)
+
+    for leftward in (0, 1):
+        @pl.when((c < 3) if leftward else (c > 0))
+        def _(leftward=leftward):
+            for j in range(2):
+                back_arrived(leftward, 0, j)
+            reduced(it_own, [it_own, back_r.at[leftward, 0]], TOK)
+
+    reduced(ig_s, [it_own], TOK)
+    ig_out = pltpu.make_async_copy(ig_s, ig_ref, local.at[4])
+    ig_out.start()
 
     across_end(sent_z)
     payload = jnp.stack([added([zb[i, j] for j in range(4)]) for i in range(2)])

time: 126 us -> 126 us (level)
  no operation moved by 1% of the time
where the time goes in v4:
time: 126 us
  Pallas kernels  125 us (99%)
    pallas_call x1, Pallas kernels, fused(): pl.pallas_call(kernel, out_shape=(jax.ShapeDtypeStruct((TOK, BLK), BF16),...  123 us

profile of v4, /device:TPU:1, one launch (start us, length us, event | category | flops | bytes accessed | tf_op | source)
XLA Modules:
  0.0 125.9 jit_solution(4657880792556530775)
XLA Ops:
  0.6 123.2 %shard_map.135 = (bf16[384,512]{1,0:T(8,128)(2,1)}, f32[64,1024]{1,0:T(8,128)}, f32[64,1024]{1,0:T(8,128)}, f32[1,64]{1,0:T(1,128)}, f32[1,1024]{1,0:T(1,128)}, /*index=5*/f32[1,1024]{1,0:T(1,128)}, f32[1,64]{1,0:T(1,128)}) custom-call(bf16[384,512]{1,0:T(8,128)(2,1)} %x_ref.1, bf16[384,512]{1,0:T(8,128)(2,1)} %cot_ref.1, bf16[64,1024]{1,0:T(8,128)(2,1)} %win_ref.1, ...), custom_call_target="tpu_custom_call" | custom-call | flops 8053063680 | bytes 16777216 | tf_op jit(solution)/shard_map/pallas_call | solution.py:639
  123.8 2.1 %shard_map.136 = (bf16[384,512]{1,0:T(8,128)(2,1)}, f32[64,1024]{1,0:T(8,128)}, f32[64,1024]{1,0:T(8,128)}, f32[1,64]{1,0:T(1,128)}, f32[1,1024]{1,0:T(1,128)}, /*index=5*/f32[1,1024]{1,0:T(1,128)}, f32[1,64]{1,0:T(1,128)}) custom-call(bf16[384,512]{1,0:T(8,128)(2,1)} %get-tuple-element.21.refs_0_, f32[64,1024]{1,0:T(8,128)} %get-tuple-element.22.refs_1_, ...), custom_call_target="tpu_custom_call" | custom-call | tf_op jit(solution)/shard_map/pallas_call | solution.py:706

commit v5 on v4

--- a/solution.py
+++ b/solution.py
@@ -20,8 +20,8 @@
 ENTRIES = WIDTH * ALL_UNITS
 
 CORE_G, STAGE1, STAGE2, DP, SUMS, SWAP, MOM = 0, 8, 20, 32, 40, 80, 82
-W_SWAP, W_RING1, W_RING2, W_PART, LINE, BACK = 83, 85, 89, 105, 121, 145
-N_SEM = 157
+W_SWAP, W_RING1, W_RING2, W_PART, LINE, BACK = 83, 85, 89, 105, 121, 133
+N_SEM = 145
 CHUNKS = ((0, 256), (256, 128), (0, 384))
 
 
@@ -132,15 +132,15 @@
             device_id=partner, device_id_type=MESH,
         ).wait_recv()
 
-    def line_number(leftward, k, i, j):
-        return LINE + ((leftward * 3 + k - 1) * 2 + j) * 2 + i
-
-    def line_copy(leftward, k, i, j):
-        rows = pl.ds(*CHUNKS[j])
+    def line_number(leftward, k, j):
+        return LINE + (leftward * 3 + k - 1) * 2 + j
+
+    def line_copy(leftward, k, j):
         owner = c + (k - 1) if leftward else c - (k - 1)
-        number = line_number(leftward, k, i, j)
+        number = line_number(leftward, k, j)
+        block = full.at[:, owner, pl.ds(*CHUNKS[j]), :]
         return pltpu.make_async_remote_copy(
-            src_ref=full.at[i, owner, rows, :], dst_ref=full.at[i, owner, rows, :], send_sem=ss.at[number], recv_sem=rs.at[number],
+            src_ref=block, dst_ref=block, send_sem=ss.at[number], recv_sem=rs.at[number],
             device_id={"col": ring(c, 3 if leftward else 1)}, device_id_type=MESH,
         )
 
@@ -154,21 +154,19 @@
         for leftward in (0, 1):
             @pl.when(line_sends(leftward, k))
             def _(leftward=leftward):
-                for i in range(2):
-                    line_copy(leftward, k, i, j).start()
+                line_copy(leftward, k, j).start()
 
     def hand_on(k, j):
-        for i in range(2):
-            for leftward in (0, 1):
-                @pl.when(line_gets(leftward, k))
-                def _(i=i, leftward=leftward):
-                    owner = c + k if leftward else c - k
-                    arrived(full.at[i, owner, pl.ds(*CHUNKS[j]), :], line_number(leftward, k, i, j))
-
-                if k < 3:
-                    @pl.when(line_sends(leftward, k + 1))
-                    def _(i=i, leftward=leftward):
-                        line_copy(leftward, k + 1, i, j).start()
+        for leftward in (0, 1):
+            @pl.when(line_gets(leftward, k))
+            def _(leftward=leftward):
+                owner = c + k if leftward else c - k
+                arrived(full.at[:, owner, pl.ds(*CHUNKS[j]), :], line_number(leftward, k, j))
+
+            if k < 3:
+                @pl.when(line_sends(leftward, k + 1))
+                def _(leftward=leftward):
+                    line_copy(leftward, k + 1, j).start()
 
     line_start(1, 0)
 
@@ -624,8 +622,7 @@
             @pl.when(line_sends(leftward, k))
             def _(leftward=leftward, k=k):
                 for j in range(2):
-                    for i in range(2):
-                        line_copy(leftward, k, i, j).wait_send()
+                    line_copy(leftward, k, j).wait_send()
 
             @pl.when((c - k >= 0) if leftward else (c + k <= 3))
             def _(leftward=leftward, k=k):

time: 126 us -> 126 us (level)
  no operation moved by 1% of the time
where the time goes in v5:
time: 126 us; the launch traced here: 125 us
  Pallas kernels  125 us (99%)
    pallas_call x1, Pallas kernels, fused(): pl.pallas_call(kernel, out_shape=(jax.ShapeDtypeStruct((TOK, BLK), BF16),...  123 us

profile of v5, /device:TPU:1, one launch (start us, length us, event | category | flops | bytes accessed | tf_op | source)
XLA Modules:
  0.0 125.3 jit_solution(12229951521965725546)
XLA Ops:
  0.6 122.6 %shard_map.135 = (bf16[384,512]{1,0:T(8,128)(2,1)}, f32[64,1024]{1,0:T(8,128)}, f32[64,1024]{1,0:T(8,128)}, f32[1,64]{1,0:T(1,128)}, f32[1,1024]{1,0:T(1,128)}, /*index=5*/f32[1,1024]{1,0:T(1,128)}, f32[1,64]{1,0:T(1,128)}) custom-call(bf16[384,512]{1,0:T(8,128)(2,1)} %x_ref.1, bf16[384,512]{1,0:T(8,128)(2,1)} %cot_ref.1, bf16[64,1024]{1,0:T(8,128)(2,1)} %win_ref.1, ...), custom_call_target="tpu_custom_call" | custom-call | flops 8053063680 | bytes 16777216 | tf_op jit(solution)/shard_map/pallas_call | solution.py:636
  123.2 2.1 %shard_map.136 = (bf16[384,512]{1,0:T(8,128)(2,1)}, f32[64,1024]{1,0:T(8,128)}, f32[64,1024]{1,0:T(8,128)}, f32[1,64]{1,0:T(1,128)}, f32[1,1024]{1,0:T(1,128)}, /*index=5*/f32[1,1024]{1,0:T(1,128)}, f32[1,64]{1,0:T(1,128)}) custom-call(bf16[384,512]{1,0:T(8,128)(2,1)} %get-tuple-element.21.refs_0_, f32[64,1024]{1,0:T(8,128)} %get-tuple-element.22.refs_1_, ...), custom_call_target="tpu_custom_call" | custom-call | tf_op jit(solution)/shard_map/pallas_call | solution.py:703

commit v6 on v5

--- a/solution.py
+++ b/solution.py
@@ -392,7 +392,15 @@
 
     def ring1_send(piece, g, h, which, device, extra=()):
         n = 2 * piece + h
-        reduced(s1.at[g, n], chip_sum(g, n) + list(extra), BLK)
+        if (piece, g) == (0, 0):
+            reduced(s1.at[g, n], chip_sum(g, n), BLK)
+        else:
+            mine = ring(p1, offsets[g])
+            lhs = jnp.concatenate([tr[m, mine * t1 + q * t2] for q in range(4)], axis=0)
+            total = jnp.dot(lhs, act[m, :, n * 256:(n + 1) * 256], preferred_element_type=F32)
+            for part in [g_recv.at[g, n]] + list(extra):
+                total += part[...].astype(F32)
+            s1[g, n] = total.astype(BF16)
         ring1[piece, which] = start(s1.at[g, n], r1.at[which, piece], STAGE1 + 2 * which + piece, device)
 
     def first(piece):
@@ -461,20 +469,15 @@
     group_theirs(0, 1)
     group_own(0, 0)
     group_theirs(0, 2)
-    group_own(0, 1)
-    group_own(0, 2)
+    group_theirs(1, 0)
     first(0)
     second(0)
-    group_theirs(1, 0)
-    group_own(1, 0)
     for k in (3, 2, 1):
         back_first(k, 1)
     third(0)
     group_theirs(1, 1)
-    group_own(1, 1)
     first(1)
     group_theirs(1, 2)
-    group_own(1, 2)
     second(1)
     group_theirs(0, 3)
     group_own(0, 3)

time: 126 us -> 126 us (level)
  no operation moved by 1% of the time
where the time goes in v6:
time: 126 us
  Pallas kernels  125 us (99%)
    pallas_call x1, Pallas kernels, fused(): pl.pallas_call(kernel, out_shape=(jax.ShapeDtypeStruct((TOK, BLK), BF16),...  123 us

profile of v6, /device:TPU:1, one launch (start us, length us, event | category | flops | bytes accessed | tf_op | source)
XLA Modules:
  0.0 125.7 jit_solution(15128496318483377530)
XLA Ops:
  0.6 122.9 %shard_map.135 = (bf16[384,512]{1,0:T(8,128)(2,1)}, f32[64,1024]{1,0:T(8,128)}, f32[64,1024]{1,0:T(8,128)}, f32[1,64]{1,0:T(1,128)}, f32[1,1024]{1,0:T(1,128)}, /*index=5*/f32[1,1024]{1,0:T(1,128)}, f32[1,64]{1,0:T(1,128)}) custom-call(bf16[384,512]{1,0:T(8,128)(2,1)} %x_ref.1, bf16[384,512]{1,0:T(8,128)(2,1)} %cot_ref.1, bf16[64,1024]{1,0:T(8,128)(2,1)} %win_ref.1, ...), custom_call_target="tpu_custom_call" | custom-call | flops 8053063680 | bytes 16777216 | tf_op jit(solution)/shard_map/pallas_call | solution.py:639
  123.5 2.1 %shard_map.136 = (bf16[384,512]{1,0:T(8,128)(2,1)}, f32[64,1024]{1,0:T(8,128)}, f32[64,1024]{1,0:T(8,128)}, f32[1,64]{1,0:T(1,128)}, f32[1,1024]{1,0:T(1,128)}, /*index=5*/f32[1,1024]{1,0:T(1,128)}, f32[1,64]{1,0:T(1,128)}) custom-call(bf16[384,512]{1,0:T(8,128)(2,1)} %get-tuple-element.21.refs_0_, f32[64,1024]{1,0:T(8,128)} %get-tuple-element.22.refs_1_, ...), custom_call_target="tpu_custom_call" | custom-call | tf_op jit(solution)/shard_map/pallas_call | solution.py:706

commit v7 on v5

--- a/solution.py
+++ b/solution.py
@@ -83,9 +83,6 @@
     peers = [{"dp": 1 - d, "col": ring(c, 2)}]
     peers += [along_z_and_cores(k) for k in range(1, 8)]
     peers += [along_xy(k) for k in range(1, 16)]
-    for peer in peers:
-        pl.semaphore_signal(barrier, inc=1, device_id=peer, device_id_type=MESH)
-
     def chip_rows(q1, q2):
         return pl.ds(pl.multiple_of((q1 * t1 + q2 * t2) * 128, 128), 128)
 
@@ -103,7 +100,11 @@
         pltpu.make_async_copy(out_row_hbm, out_row_ref, local.at[7]),
         pltpu.make_async_copy(out_col_hbm, out_col_ref, local.at[8]),
     ]
-    for copy in loads:
+    for copy in loads[:4]:
+        copy.start()
+    for peer in peers:
+        pl.semaphore_signal(barrier, inc=1, device_id=peer, device_id_type=MESH)
+    for copy in loads[4:]:
         copy.start()
     for copy in loads:
         copy.wait()
@@ -523,15 +524,15 @@
         col_sums.append(jnp.sum(squared, axis=0, keepdims=True))
         folded = squared[:, 0:128] + squared[:, 128:256]
         lanes = folded if n == 0 else lanes + folded
+    row_sums = jnp.sum(lanes.T, axis=0, keepdims=True)
+    total = jnp.sum(row_sums, axis=1, keepdims=True)
+    sub8 = lax.broadcasted_iota(jnp.int32, (8, 128), 0)
+    sent_z = across_start(za.at[c], SUMS + 15, 3, along_z, jnp.where(sub8 == 0, row_sums, old_f_sum))
     sub = lax.broadcasted_iota(jnp.int32, (8, 256), 0)
     payload = jnp.where(sub == 4, old_d_sum, 0.0)
     for n in range(4):
         payload = jnp.where(sub == n, col_sums[n], payload)
     sent_xy = across_start(xa.at[chip], SUMS, 15, along_xy, payload)
-    row_sums = jnp.sum(lanes.T, axis=0, keepdims=True)
-    total = jnp.sum(row_sums, axis=1, keepdims=True)
-    sub = lax.broadcasted_iota(jnp.int32, (8, 128), 0)
-    sent_z = across_start(za.at[c], SUMS + 15, 3, along_z, jnp.where(sub == 0, row_sums, old_f_sum))
     terms(c, 2, keep_mine(*CHUNKS[2]))
     across_end(sent_z)
     over_z = added([za[i] for i in range(4)])
@@ -554,7 +555,7 @@
     folded = lanes[0:8]
     for i in range(1, 16):
         folded += lanes[i * 8:(i + 1) * 8]
-    payload = jnp.concatenate([folded, jnp.where(sub == 0, total, old_mean)], axis=0)
+    payload = jnp.concatenate([folded, jnp.where(sub8 == 0, total, old_mean)], axis=0)
     sent_z = across_start(zb.at[core, c], SUMS + 18, 7, along_z_and_cores, payload)
 
     theirs_at = pl.ds(pl.multiple_of(other * 64, 64), 64)

time: 126 us -> 126 us (level)
  no operation moved by 1% of the time
where the time goes in v7:
time: 126 us; the launch traced here: 125 us
  Pallas kernels  125 us (99%)
    pallas_call x1, Pallas kernels, fused(): pl.pallas_call(kernel, out_shape=(jax.ShapeDtypeStruct((TOK, BLK), BF16),...  123 us

profile of v7, /device:TPU:1, one launch (start us, length us, event | category | flops | bytes accessed | tf_op | source)
XLA Modules:
  0.0 125.4 jit_solution(1337483520956407540)
XLA Ops:
  0.6 122.7 %shard_map.135 = (bf16[384,512]{1,0:T(8,128)(2,1)}, f32[64,1024]{1,0:T(8,128)}, f32[64,1024]{1,0:T(8,128)}, f32[1,64]{1,0:T(1,128)}, f32[1,1024]{1,0:T(1,128)}, /*index=5*/f32[1,1024]{1,0:T(1,128)}, f32[1,64]{1,0:T(1,128)}) custom-call(bf16[384,512]{1,0:T(8,128)(2,1)} %x_ref.1, bf16[384,512]{1,0:T(8,128)(2,1)} %cot_ref.1, bf16[64,1024]{1,0:T(8,128)(2,1)} %win_ref.1, ...), custom_call_target="tpu_custom_call" | custom-call | flops 8053063680 | bytes 16777216 | tf_op jit(solution)/shard_map/pallas_call | solution.py:637
  123.3 2.1 %shard_map.136 = (bf16[384,512]{1,0:T(8,128)(2,1)}, f32[64,1024]{1,0:T(8,128)}, f32[64,1024]{1,0:T(8,128)}, f32[1,64]{1,0:T(1,128)}, f32[1,1024]{1,0:T(1,128)}, /*index=5*/f32[1,1024]{1,0:T(1,128)}, f32[1,64]{1,0:T(1,128)}) custom-call(bf16[384,512]{1,0:T(8,128)(2,1)} %get-tuple-element.21.refs_0_, f32[64,1024]{1,0:T(8,128)} %get-tuple-element.22.refs_1_, ...), custom_call_target="tpu_custom_call" | custom-call | tf_op jit(solution)/shard_map/pallas_call | solution.py:704
